TPU v7x, 32 devices: a whole 2x2x4 slice. The times are simulated.
32 devices in a mesh: row: 4 (over y, core), col: 8 (over z, x).
Axes of the slice: x: 2, y: 2, z: 4, core: 2. Of those that a mesh axis runs over, the one named last changes fastest.
Arguments:
- queries: bfloat16 [4, 4096, 256], P(None, ('row', 'col'))
- probes: int32 [4, 4096, 2], P(None, ('row', 'col')), may hold values from 0 to 31, all different within a row; in each aligned block of 128 rows (0 to 127, 128 to 255, ..., all dimensions but the last counted through in order) at most 16 rows name the same one
- keys: bfloat16 [32, 1024, 256], P(('row', 'col')), may hold values from -6 to 6
- values: bfloat16 [32, 1024, 256], P(('row', 'col')), may hold values from -6 to 6
- bucket_home: int32 [32], replicated, may hold values from 0 to 31, each once
- bucket_rows: int32 [32], replicated, may hold values from 1 to 1024, 12288 in all
Outputs:
- attended: bfloat16 [4, 4096, 256], P(None, ('row', 'col'))
Inputs may be any that keep to these rules, and one draw needn't show every extreme that they name: `probes`: each request names two different buckets; among the requests of one device in one step no bucket is named more than 16 times, a bound that some block reaches. `bucket_home`: each device holds exactly one bucket. `bucket_rows`: some bucket fills all 8 blocks.
All inputs are finite; a program needn't handle non-finite values.
Results may differ from a plain program's by a relative error of at most 0.007.
Values may be sent and summed in bfloat16 or wider, within the bound.
A program may use at most 64 MiB of HBM per device.

v0:
```python
import math

import jax
import jax.numpy as jnp
from jax import lax
from jax.sharding import PartitionSpec as P

H = 8
HD = 32
BLK = 128


very_low = -1e30


def attend_blocks(query_rows, key_store, value_store, block_count, valid_count):
    query_count = query_rows.shape[0]
    query_heads = query_rows.reshape(query_count, H, HD)
    score_scale = 1.0 / math.sqrt(HD)

    def one_block(block_index, running_state):
        running, mass, weighted = running_state
        key_block = lax.dynamic_slice_in_dim(key_store, block_index * BLK, BLK, 0).reshape(
            BLK, H, HD
        )
        value_block = lax.dynamic_slice_in_dim(value_store, block_index * BLK, BLK, 0).reshape(
            BLK, H, HD
        )
        scores = (
            jnp.einsum("qhd,khd->qhk", query_heads, key_block, preferred_element_type=jnp.float32)
            * score_scale
        )
        row_index = block_index * BLK + lax.iota(jnp.int32, BLK)
        scores = jnp.where((row_index < valid_count)[None, None, :], scores, very_low)
        fresh = jnp.maximum(running, jnp.max(scores, axis=-1))
        factor = jnp.exp(running - fresh)
        weights = jnp.exp(scores - fresh[:, :, None])
        mass = mass * factor + jnp.sum(weights, axis=-1)
        weighted = weighted * factor[:, :, None] + jnp.einsum(
            "qhk,khd->qhd",
            weights.astype(jnp.bfloat16),
            value_block,
            preferred_element_type=jnp.float32,
        )
        return (fresh, mass, weighted)

    start_state = (
        jnp.full((query_count, H), very_low, jnp.float32),
        jnp.zeros((query_count, H), jnp.float32),
        jnp.zeros((query_count, H, HD), jnp.float32),
    )
    running, mass, weighted = lax.fori_loop(0, block_count, one_block, start_state)
    has_mass = mass > 0.0
    safe_mass = jnp.where(has_mass, mass, 1.0)
    log_mass = jnp.where(has_mass, running + jnp.log(safe_mass), very_low)
    partial_out = (weighted / safe_mass[:, :, None]).reshape(query_count, H * HD)
    return (partial_out, log_mass)


def send_requests(buffer):
    return lax.all_to_all(buffer, ("row", "col"), split_axis=0, concat_axis=0, tiled=True)


def return_answers(partials, masses):
    return (
        lax.all_to_all(partials, ("row", "col"), split_axis=0, concat_axis=0, tiled=True),
        lax.all_to_all(masses, ("row", "col"), split_axis=0, concat_axis=0, tiled=True),
    )


def pick_device(table, device_ids, device):
    return jnp.sum(jnp.where(device_ids == device, table, 0))


def body(queries, probes, keys, values, bucket_home, bucket_rows):
    row_count = lax.axis_size("row")
    col_count = lax.axis_size("col")
    bucket_count = row_count * col_count
    per_device = queries.shape[1]
    capacity = max(2, 4 * per_device // bucket_count)
    width = queries.shape[2]
    device_self = lax.axis_index(("row", "col"))
    device_ids = lax.iota(jnp.int32, bucket_count)
    home_match = (bucket_home[None, :] == device_ids[:, None]).astype(jnp.int32)
    device_rows = jnp.sum(home_match * bucket_rows[None, :], axis=1)
    device_blocks = (device_rows + BLK - 1) // BLK
    key_store = keys[0]
    value_store = values[0]
    my_rows = pick_device(device_rows, device_ids, device_self)
    my_blocks = pick_device(device_blocks, device_ids, device_self)
    results = []
    for round_index in range(queries.shape[0]):
        query_now = queries[round_index]
        probe_ids = probes[round_index].reshape(2 * per_device)
        bucket_match = (probe_ids[:, None] == device_ids[None, :]).astype(jnp.int32)
        earlier = jnp.cumsum(bucket_match, axis=0) - bucket_match
        order_in = jnp.sum(earlier * bucket_match, axis=1)
        target = jnp.sum(bucket_match * bucket_home[None, :], axis=1)
        first_pos = target * capacity + order_in
        paired = jnp.repeat(query_now, 2, axis=0)
        outgoing = (
            jnp.zeros((bucket_count * capacity, width), jnp.bfloat16)
            .at[first_pos]
            .set(paired, mode="drop")
        )
        incoming = send_requests(outgoing.reshape(bucket_count, capacity, width))
        own_rows = incoming.reshape(bucket_count * capacity, width)
        own_out, own_mass = attend_blocks(own_rows, key_store, value_store, my_blocks, my_rows)
        partials = own_out.reshape(bucket_count, capacity, width)
        masses = own_mass.reshape(bucket_count, capacity, H)
        back_out, back_mass = return_answers(partials, masses)
        back_out = back_out.reshape(bucket_count * capacity, width)
        back_mass = back_mass.reshape(bucket_count * capacity, H)
        gathered_out = back_out[first_pos].reshape(per_device, 2, H, HD)
        gathered_mass = back_mass[first_pos].reshape(per_device, 2, H)
        highest = jnp.max(gathered_mass, axis=1, keepdims=True)
        shares = jnp.exp(gathered_mass - highest)
        shares = shares / jnp.sum(shares, axis=1, keepdims=True)
        merged = jnp.sum(shares[:, :, :, None] * gathered_out, axis=1)
        results.append(merged.reshape(per_device, width).astype(jnp.bfloat16))
    return jnp.stack(results, axis=0)


def solution(mesh):
    return jax.shard_map(
        body,
        mesh=mesh,
        in_specs=(
            P(None, ("row", "col"), None),
            P(None, ("row", "col"), None),
            P(("row", "col"), None, None),
            P(("row", "col"), None, None),
            P(),
            P(),
        ),
        out_specs=P(None, ("row", "col"), None),
        check_vma=False,
    )
```

profile of v0, /device:TPU:0, one launch (start us, length us, event | category | flops | bytes accessed | tf_op | source)
XLA Modules:
  0.0 275.2 jit_solution(7359384485757142526)
XLA Ops:
  7.7 2.1 scatter_custom_fusion
  9.8 7.3 %all-to-all-start = ((bf16[32,16,256]{2,1,0:T(8,128)(2,1)}), bf16[32,16,256]{2,1,0:T(8,128)(2,1)S(1)}, u32[]{:S(2)}, u32[]{:S(2)}) async-start(bf16[32,16,256]{2,1,0:T(8,128)(2,1)} %bitcast.21), calls=%async_computation | async-start | bytes 524288 | tf_op jit(solution)/shard_map/all_to_all | solution.py:61
  18.1 2.1 scatter_custom_fusion.1
  20.2 2.1 scatter_custom_fusion.2
  22.3 2.2 scatter_custom_fusion.3
  25.3 2.4 all-to-all-done
  27.8 3.4 %all-to-all-start.3 = ((bf16[32,16,256]{2,1,0:T(8,128)(2,1)}), bf16[32,16,256]{2,1,0:T(8,128)(2,1)S(1)}, u32[]{:S(2)}, u32[]{:S(2)}) async-start(bf16[32,16,256]{2,1,0:T(8,128)(2,1)} %bitcast.31), calls=%async_computation.3 | async-start | bytes 524288 | tf_op jit(solution)/shard_map/all_to_all | solution.py:61
  32.4 3.8 %while.56 = (s32[]{:T(128)}, f32[512,8]{0,1:T(8,128)S(1)}, f32[512,8]{0,1:T(8,128)S(1)}, f32[512,8,32]{0,2,1:T(8,128)S(1)}, s32[]{:T(128)}, /*index=5*/s32[]{:T(...) while((s32[]{:T(128)}, f32[512,8]{0,1:T(8,128)S(1)}, ...), condition=%wide.region_11.12_spmd, body=%wide.region_8.11_spmd.sunk | while | flops 73146624 | bytes 8258231 | solution.py:52
  36.2 5.6 %all-to-all-done.3 = bf16[32,16,256]{2,1,0:T(8,128)(2,1)S(1)} async-done(((bf16[32,16,256]{2,1,0:T(8,128)(2,1)}), bf16[32,16,256]{2,1,0:T(8,128)(2,1)S(1)}, u32[]{:S(2)}, u32[]{:S(2)}) %all-to-all-start.3) | async-done | bytes 262176 | tf_op jit(solution)/shard_map/all_to_all | solution.py:61
  42.5 21.5 %all-to-all-start.6 = ((bf16[32,16,256]{2,1,0:T(8,128)(2,1)}), bf16[32,16,256]{2,1,0:T(8,128)(2,1)}, u32[]{:S(2)}, u32[]{:S(2)}) async-start(bf16[32,16,256]{2,1,0:T(8,128)(2,1)} %bitcast.40), calls=%async_computation.6 | async-start | bytes 524288 | tf_op jit(solution)/shard_map/all_to_all | solution.py:61
  64.1 1.7 reshape_reshape.26
  66.5 3.8 %while.57 = (s32[]{:T(128)}, f32[512,8]{0,1:T(8,128)S(1)}, f32[512,8]{0,1:T(8,128)S(1)}, f32[512,8,32]{0,2,1:T(8,128)S(1)}, s32[]{:T(128)}, /*index=5*/s32[]{:T(...) while((s32[]{:T(128)}, f32[512,8]{0,1:T(8,128)S(1)}, ...), condition=%wide.region_23.24_spmd, body=%wide.region_20.23_spmd.sunk | while | flops 73146624 | bytes 8258231 | solution.py:52
  70.3 4.2 %all-to-all-done.6 = bf16[32,16,256]{2,1,0:T(8,128)(2,1)} async-done(((bf16[32,16,256]{2,1,0:T(8,128)(2,1)}), bf16[32,16,256]{2,1,0:T(8,128)(2,1)}, u32[]{:S(2)}, u32[]{:S(2)}) %all-to-all-start.6) | async-done | bytes 262176 | tf_op jit(solution)/shard_map/all_to_all | solution.py:61
  74.5 22.4 %all-to-all-start.9 = ((bf16[32,16,256]{2,1,0:T(8,128)(2,1)}), bf16[32,16,256]{2,1,0:T(8,128)(2,1)S(1)}, u32[]{:S(2)}, u32[]{:S(2)}) async-start(bf16[32,16,256]{2,1,0:T(8,128)(2,1)} %bitcast.49), calls=%async_computation.9 | async-start | bytes 524288 | tf_op jit(solution)/shard_map/all_to_all | solution.py:61
  97.0 2.5 reshape_reshape.28
  99.4 1.8 copy.159
  101.3 3.8 %while.58 = (s32[]{:T(128)}, f32[512,8]{0,1:T(8,128)S(1)}, f32[512,8]{0,1:T(8,128)S(1)}, f32[512,8,32]{0,2,1:T(8,128)S(1)}, s32[]{:T(128)}, /*index=5*/s32[]{:T(...) while((s32[]{:T(128)}, f32[512,8]{0,1:T(8,128)S(1)}, ...), condition=%wide.region_35.36_spmd, body=%wide.region_32.35_spmd.sunk | while | flops 73146624 | bytes 8258231 | solution.py:52
  106.0 1.6 all-to-all-done.9
  107.6 25.3 %all-to-all-start.1 = ((f32[32,1,128]{2,1,0:T(1,128)}), f32[32,1,128]{2,1,0:T(1,128)S(1)}, u32[]{:S(2)}, u32[]{:S(2)}) async-start(f32[32,1,128]{2,1,0:T(1,128)} %reshape.544), calls=%async_computation.1 | async-start | bytes 32768 | tf_op jit(solution)/shard_map/all_to_all | solution.py:67
  132.9 1.4 reshape_reshape.30
  134.3 1.8 copy.167
  136.3 3.8 %while.59 = (s32[]{:T(128)}, f32[512,8]{0,1:T(8,128)S(1)}, f32[512,8]{0,1:T(8,128)S(1)}, f32[512,8,32]{0,2,1:T(8,128)S(1)}, s32[]{:T(128)}, /*index=5*/s32[]{:T(...) while((s32[]{:T(128)}, f32[512,8]{0,1:T(8,128)S(1)}, ...), condition=%wide.region_47.48_spmd, body=%wide.region_44.47_spmd.sunk | while | flops 73146624 | bytes 8258231 | solution.py:52
  141.0 26.8 %all-to-all-start.4 = ((f32[32,1,128]{2,1,0:T(1,128)}), f32[32,1,128]{2,1,0:T(1,128)S(1)}, u32[]{:S(2)}, u32[]{:S(2)}) async-start(f32[32,1,128]{2,1,0:T(1,128)} %reshape.542), calls=%async_computation.4 | async-start | bytes 32768 | tf_op jit(solution)/shard_map/all_to_all | solution.py:67
  168.7 6.1 %all-to-all-done.4 = f32[32,1,128]{2,1,0:T(1,128)S(1)} async-done(((f32[32,1,128]{2,1,0:T(1,128)}), f32[32,1,128]{2,1,0:T(1,128)S(1)}, u32[]{:S(2)}, u32[]{:S(2)}) %all-to-all-start.4) | async-done | bytes 16416 | tf_op jit(solution)/shard_map/all_to_all | solution.py:67
  174.9 2.6 all-to-all-start.7
  178.4 6.2 %all-to-all-done.7 = f32[32,1,128]{2,1,0:T(1,128)S(1)} async-done(((f32[32,1,128]{2,1,0:T(1,128)}), f32[32,1,128]{2,1,0:T(1,128)S(1)}, u32[]{:S(2)}, u32[]{:S(2)}) %all-to-all-start.7) | async-done | bytes 16416 | tf_op jit(solution)/shard_map/all_to_all | solution.py:67
  184.5 2.5 all-to-all-start.10
  187.2 2.0 copy.146
  189.1 2.8 %reshape_reshape.25 = f32[32,16,256]{2,1,0:T(8,128)} reshape(f32[512,8,32]{2,1,0:T(8,128)} %copy.146) | data formatting | bytes 1048576 | tf_op jit(solution)/shard_map/reshape;reshape | solution.py:109
  191.9 2.2 all-to-all-done.10
  194.1 3.8 %all-to-all-start.2 = ((f32[32,16,256]{2,1,0:T(8,128)}), f32[32,16,256]{2,1,0:T(8,128)S(1)}, u32[]{:S(2)}, u32[]{:S(2)}) async-start(f32[32,16,256]{2,1,0:T(8,128)} %reshape_reshape.25), calls=%async_computation.2 | async-start | bytes 1048576 | tf_op jit(solution)/shard_map/all_to_all | solution.py:66
  198.0 2.0 copy.154
  200.0 2.8 %reshape_reshape.27 = f32[32,16,256]{2,1,0:T(8,128)} reshape(f32[512,8,32]{2,1,0:T(8,128)} %copy.154) | data formatting | bytes 1048576 | tf_op jit(solution)/shard_map/reshape;reshape | solution.py:109
  202.8 11.3 %all-to-all-done.2 = f32[32,16,256]{2,1,0:T(8,128)S(1)} async-done(((f32[32,16,256]{2,1,0:T(8,128)}), f32[32,16,256]{2,1,0:T(8,128)S(1)}, u32[]{:S(2)}, u32[]{:S(2)}) %all-to-all-start.2) | async-done | bytes 524320 | tf_op jit(solution)/shard_map/all_to_all | solution.py:66
  214.1 2.6 all-to-all-start.5
  216.8 2.0 copy.162
  218.8 2.8 %reshape_reshape.29 = f32[32,16,256]{2,1,0:T(8,128)} reshape(f32[512,8,32]{2,1,0:T(8,128)} %copy.162) | data formatting | bytes 1048576 | tf_op jit(solution)/shard_map/reshape;reshape | solution.py:109
  221.6 11.5 %all-to-all-done.5 = f32[32,16,256]{2,1,0:T(8,128)S(1)} async-done(((f32[32,16,256]{2,1,0:T(8,128)}), f32[32,16,256]{2,1,0:T(8,128)S(1)}, u32[]{:S(2)}, u32[]{:S(2)}) %all-to-all-start.5) | async-done | bytes 524320 | tf_op jit(solution)/shard_map/all_to_all | solution.py:66
  233.1 2.6 all-to-all-start.8
  235.8 2.0 copy.170
  237.7 2.8 %reshape_reshape.31 = f32[32,16,256]{2,1,0:T(8,128)} reshape(f32[512,8,32]{2,1,0:T(8,128)} %copy.170) | data formatting | bytes 1048576 | tf_op jit(solution)/shard_map/reshape;reshape | solution.py:109
  249.1 1.0 gather_fusion.1
  250.4 1.7 all-to-all-done.8
  252.0 4.2 %all-to-all-start.11 = ((f32[32,16,256]{2,1,0:T(8,128)}), f32[32,16,256]{2,1,0:T(8,128)S(1)}, u32[]{:S(2)}, u32[]{:S(2)}) async-start(f32[32,16,256]{2,1,0:T(8,128)} %reshape_reshape.31), calls=%async_computation.11 | async-start | bytes 1048576 | tf_op jit(solution)/shard_map/all_to_all | solution.py:66
  256.8 1.0 gather_fusion.3
  258.5 1.0 gather_fusion.5
  260.3 12.3 %all-to-all-done.11 = f32[32,16,256]{2,1,0:T(8,128)S(1)} async-done(((f32[32,16,256]{2,1,0:T(8,128)}), f32[32,16,256]{2,1,0:T(8,128)S(1)}, u32[]{:S(2)}, u32[]{:S(2)}) %all-to-all-start.11) | async-done | bytes 524320 | tf_op jit(solution)/shard_map/all_to_all | solution.py:66
  272.6 1.0 gather_fusion.7
  (170 shorter events, 38.1 us)
Async XLA Ops:
  0.0 17.2 %copy-start.1 = (bf16[1,1024,256]{2,1,0:T(8,128)(2,1)S(1)}, bf16[1,1024,256]{2,1,0:T(8,128)(2,1)}, u32[]{:S(2)}) copy-start(bf16[1,1024,256]{2,1,0:T(8,128)(2,1)} %param.16) | copy-start | bytes 1572868
  1.2 16.2 %copy-start.2 = (bf16[1,1024,256]{2,1,0:T(8,128)(2,1)S(1)}, bf16[1,1024,256]{2,1,0:T(8,128)(2,1)}, u32[]{:S(2)}) copy-start(bf16[1,1024,256]{2,1,0:T(8,128)(2,1)} %param.17) | copy-start | bytes 1572868
  9.8 18.0 %all-to-all-start = ((bf16[32,16,256]{2,1,0:T(8,128)(2,1)}), bf16[32,16,256]{2,1,0:T(8,128)(2,1)S(1)}, u32[]{:S(2)}, u32[]{:S(2)}) async-start(bf16[32,16,256]{2,1,0:T(8,128)(2,1)} %bitcast.21), calls=%async_computation | async-start | bytes 524288 | tf_op jit(solution)/shard_map/all_to_all | solution.py:61
  17.2 7.3 %copy-start.3 = (s32[32]{0:T(128)S(1)}, s32[32]{0:T(128)}, u32[]{:S(2)}) copy-start(s32[32]{0:T(128)} %param.18) | copy-start | bytes 388
  17.2 7.3 %copy-start.4 = (s32[32]{0:T(128)S(1)}, s32[32]{0:T(128)}, u32[]{:S(2)}) copy-start(s32[32]{0:T(128)} %param.19) | copy-start | bytes 388
  27.8 14.1 %all-to-all-start.3 = ((bf16[32,16,256]{2,1,0:T(8,128)(2,1)}), bf16[32,16,256]{2,1,0:T(8,128)(2,1)S(1)}, u32[]{:S(2)}, u32[]{:S(2)}) async-start(bf16[32,16,256]{2,1,0:T(8,128)(2,1)} %bitcast.31), calls=%async_computation.3 | async-start | bytes 524288 | tf_op jit(solution)/shard_map/all_to_all | solution.py:61
  41.8 0.7 copy-start
  42.5 32.0 %all-to-all-start.6 = ((bf16[32,16,256]{2,1,0:T(8,128)(2,1)}), bf16[32,16,256]{2,1,0:T(8,128)(2,1)}, u32[]{:S(2)}, u32[]{:S(2)}) async-start(bf16[32,16,256]{2,1,0:T(8,128)(2,1)} %bitcast.40), calls=%async_computation.6 | async-start | bytes 524288 | tf_op jit(solution)/shard_map/all_to_all | solution.py:61
  74.5 33.1 %all-to-all-start.9 = ((bf16[32,16,256]{2,1,0:T(8,128)(2,1)}), bf16[32,16,256]{2,1,0:T(8,128)(2,1)S(1)}, u32[]{:S(2)}, u32[]{:S(2)}) async-start(bf16[32,16,256]{2,1,0:T(8,128)(2,1)} %bitcast.49), calls=%async_computation.9 | async-start | bytes 524288 | tf_op jit(solution)/shard_map/all_to_all | solution.py:61
  107.6 33.4 %all-to-all-start.1 = ((f32[32,1,128]{2,1,0:T(1,128)}), f32[32,1,128]{2,1,0:T(1,128)S(1)}, u32[]{:S(2)}, u32[]{:S(2)}) async-start(f32[32,1,128]{2,1,0:T(1,128)} %reshape.544), calls=%async_computation.1 | async-start | bytes 32768 | tf_op jit(solution)/shard_map/all_to_all | solution.py:67
  141.0 33.9 %all-to-all-start.4 = ((f32[32,1,128]{2,1,0:T(1,128)}), f32[32,1,128]{2,1,0:T(1,128)S(1)}, u32[]{:S(2)}, u32[]{:S(2)}) async-start(f32[32,1,128]{2,1,0:T(1,128)} %reshape.542), calls=%async_computation.4 | async-start | bytes 32768 | tf_op jit(solution)/shard_map/all_to_all | solution.py:67
  174.9 9.7 %all-to-all-start.7 = ((f32[32,1,128]{2,1,0:T(1,128)}), f32[32,1,128]{2,1,0:T(1,128)S(1)}, u32[]{:S(2)}, u32[]{:S(2)}) async-start(f32[32,1,128]{2,1,0:T(1,128)} %reshape.540), calls=%async_computation.7 | async-start | bytes 32768 | tf_op jit(solution)/shard_map/all_to_all | solution.py:67
  184.5 9.6 %all-to-all-start.10 = ((f32[32,1,128]{2,1,0:T(1,128)}), f32[32,1,128]{2,1,0:T(1,128)S(1)}, u32[]{:S(2)}, u32[]{:S(2)}) async-start(f32[32,1,128]{2,1,0:T(1,128)} %reshape.538), calls=%async_computation.10 | async-start | bytes 32768 | tf_op jit(solution)/shard_map/all_to_all | solution.py:67
  194.1 20.0 %all-to-all-start.2 = ((f32[32,16,256]{2,1,0:T(8,128)}), f32[32,16,256]{2,1,0:T(8,128)S(1)}, u32[]{:S(2)}, u32[]{:S(2)}) async-start(f32[32,16,256]{2,1,0:T(8,128)} %reshape_reshape.25), calls=%async_computation.2 | async-start | bytes 1048576 | tf_op jit(solution)/shard_map/all_to_all | solution.py:66
  214.1 19.0 %all-to-all-start.5 = ((f32[32,16,256]{2,1,0:T(8,128)}), f32[32,16,256]{2,1,0:T(8,128)S(1)}, u32[]{:S(2)}, u32[]{:S(2)}) async-start(f32[32,16,256]{2,1,0:T(8,128)} %reshape_reshape.27), calls=%async_computation.5 | async-start | bytes 1048576 | tf_op jit(solution)/shard_map/all_to_all | solution.py:66
  233.1 19.0 %all-to-all-start.8 = ((f32[32,16,256]{2,1,0:T(8,128)}), f32[32,16,256]{2,1,0:T(8,128)S(1)}, u32[]{:S(2)}, u32[]{:S(2)}) async-start(f32[32,16,256]{2,1,0:T(8,128)} %reshape_reshape.29), calls=%async_computation.8 | async-start | bytes 1048576 | tf_op jit(solution)/shard_map/all_to_all | solution.py:66
  252.0 20.5 %all-to-all-start.11 = ((f32[32,16,256]{2,1,0:T(8,128)}), f32[32,16,256]{2,1,0:T(8,128)S(1)}, u32[]{:S(2)}, u32[]{:S(2)}) async-start(f32[32,16,256]{2,1,0:T(8,128)} %reshape_reshape.31), calls=%async_computation.11 | async-start | bytes 1048576 | tf_op jit(solution)/shard_map/all_to_all | solution.py:66
where the time goes:
time: 277 us; the launch traced here: 275 us
  starting transfers between devices  125 us (45%)
  waiting for transfers between devices  65.1 us (24%)
  local copies, waits for them, and re-layouts  59.2 us (21%)
  other arithmetic  14.7 us (5%)
  loops' own time  5.4 us (2%)
  matrix products  4.96 us (2%)
    all_to_all x4, starting transfers between devices, return_answers(): lax.all_to_all(masses, ('row', 'col'), split_axis=0, concat_axis=0, tiled...  57.2 us
    all_to_all x4, starting transfers between devices, send_requests(): lax.all_to_all(buffer, ('row', 'col'), split_axis=0, concat_axis=0, tiled...  54.7 us
    all_to_all x4, waiting for transfers between devices, return_answers(): lax.all_to_all(partials, ('row', 'col'), split_axis=0, concat_axis=0, til...  36.7 us
    all_to_all x4, waiting for transfers between devices, return_answers(): lax.all_to_all(masses, ('row', 'col'), split_axis=0, concat_axis=0, tiled...  14.5 us
    all_to_all x4, waiting for transfers between devices, send_requests(): lax.all_to_all(buffer, ('row', 'col'), split_axis=0, concat_axis=0, tiled...  13.8 us
    all_to_all x4, starting transfers between devices, return_answers(): lax.all_to_all(partials, ('row', 'col'), split_axis=0, concat_axis=0, til...  13.2 us
    another operation x4, local copies, waits for them, and re-layouts, body(): partials = own_out.reshape(bucket_count, capacity, width)  11 us
    scatter x4, local copies, waits for them, and re-layouts, body(): outgoing = jnp.zeros((bucket_count * capacity, width), jnp.bfloat16).at[f...  8.58 us
  transfers between devices with their start and end apart: 12, of which 11 were waited for; matrix products, arithmetic and copies ran while one was open for 24% of the time, Pallas kernels for 0%

commit v1 on v0

v1 whole, which is shorter than its diff:
```python
import functools
import math

import jax
import jax.numpy as jnp
from jax import lax
from jax.experimental import pallas as pl
from jax.experimental.pallas import tpu as pltpu
from jax.sharding import PartitionSpec as P

HD = 32
LANES = 128
ROWS = 16
TILE = 256
MESH = pl.DeviceIdType.MESH
bf16 = jnp.bfloat16
f32 = jnp.float32


def iota(shape, dim):
    return lax.broadcasted_iota(jnp.int32, shape, dim)


def kernel(
    dims, q_ref, probe_ref, home_ref, rows_ref, k_ref, v_ref, out_ref,
    keys_by_head, values_by_head, pos_ref, send, recv, back, answer, mass_back, mass_answer,
    send_sem, recv_sem, back_sem, answer_sem, mass_back_sem, mass_answer_sem,
):
    n, ncol, steps, nq, width, cap, per_phase, phases = dims
    heads = width // HD
    key_rows = k_ref.shape[0]
    slots = n * ROWS
    scale = math.log2(math.e) / math.sqrt(HD)
    me = lax.axis_index("row") * ncol + lax.axis_index("col")

    def peer(index):
        other = lax.rem(me + index, n)
        return other, (other // ncol, lax.rem(other, ncol))

    barrier = pltpu.get_barrier_semaphore()

    @pl.loop(1, n)
    def _(index):
        _, where = peer(index)
        pl.semaphore_signal(barrier, inc=1, device_id=where, device_id_type=MESH)

    def copy_to(index, phase, source, target, source_sem, target_sem):
        other, where = peer(index)
        return pltpu.make_async_remote_copy(
            src_ref=source.at[phase, other],
            dst_ref=target.at[phase, me],
            send_sem=source_sem.at[phase],
            recv_sem=target_sem.at[phase],
            device_id=where,
            device_id_type=MESH,
        )

    def all_copies(phase, source, target, source_sem, target_sem):
        _, where = peer(1)
        return pltpu.make_async_remote_copy(
            src_ref=source.at[phase, pl.ds(0, n - 1)],
            dst_ref=target.at[phase, pl.ds(0, n - 1)],
            send_sem=source_sem.at[phase],
            recv_sem=target_sem.at[phase],
            device_id=where,
            device_id_type=MESH,
        )

    queries_out = (send, recv, send_sem, recv_sem)
    answers_out = (back, answer, back_sem, answer_sem)
    masses_out = (mass_back, mass_answer, mass_back_sem, mass_answer_sem)

    home_row = home_ref[...]
    diagonal = iota((n, n), 0) == iota((n, n), 1)
    home_column = jnp.sum(jnp.where(diagonal, home_row, 0), axis=1, keepdims=True).astype(f32)
    before = (iota((nq, nq), 0) < iota((nq, nq), 1)).astype(bf16)

    def slot_rows(step):
        ids = probe_ref[step]
        first = (iota((n, nq), 0) == ids[0:1, :]).astype(f32)
        second = (iota((n, nq), 0) == ids[1:2, :]).astype(f32)
        both = jnp.concatenate([first, second], axis=0).astype(bf16)
        earlier = jnp.dot(both, before, preferred_element_type=f32)
        offset = jnp.sum(first, axis=1, keepdims=True)
        order_first = jnp.sum(first * (earlier[:n] + home_column * ROWS), axis=0, keepdims=True)
        order_second = jnp.sum(
            second * (earlier[n:] + offset + home_column * ROWS), axis=0, keepdims=True
        )
        shift = (step % per_phase) * cap
        return jnp.concatenate([order_first, order_second], axis=0).astype(jnp.int32) + shift

    def arrange(phase):
        total = None
        for local in range(per_phase):
            step = phase * per_phase + local
            pos = slot_rows(step)
            pos_ref[step] = pos
            places = iota((slots, nq), 0)
            match = ((places == pos[0:1, :]) | (places == pos[1:2, :])).astype(f32).astype(bf16)
            part = jnp.dot(match, q_ref[step], preferred_element_type=f32)
            total = part if total is None else total + part
        send[phase] = total.astype(bf16).reshape(n, ROWS, width)

    for phase in range(phases):
        arrange(phase)
        if phase == 0:
            pl.semaphore_wait(barrier, n - 1)

        @pl.loop(1, n)
        def _(index):
            copy_to(index, phase, *queries_out).start()

    mine = jnp.sum(jnp.where(home_row == me, rows_ref[...], 0), axis=1, keepdims=True)
    valid = iota((key_rows, width), 0) < mine
    keys_all = k_ref[...].astype(f32)
    keys_all = jnp.where(valid, keys_all, keys_all[0:1, :]).T
    values_all = jnp.where(valid, v_ref[...].astype(f32), 0.0)
    counted = jnp.where(valid, 1.0, 0.0)
    for head in range(heads):
        keys_by_head[head] = jnp.where(
            iota((width, key_rows), 0) // HD == head, keys_all, 0.0
        ).astype(bf16)
        values_by_head[head] = jnp.where(
            iota((key_rows, width), 1) // HD == head, values_all, counted
        ).astype(bf16)

    lane = iota((TILE, LANES), 1)
    group = LANES // HD

    def attend(phase, tile):
        devices = TILE // ROWS
        start = pl.multiple_of(tile * devices, devices)
        queries = recv[phase, pl.ds(start, devices)].reshape(TILE, width)
        halves = [jnp.zeros((TILE, LANES), f32) for _ in range(width // LANES)]
        masses = jnp.ones((TILE, LANES), f32)
        tops = jnp.zeros((TILE, LANES), f32)
        for head in range(heads):
            scores = jnp.dot(queries, keys_by_head[head], preferred_element_type=f32)
            top = jnp.max(scores, axis=1, keepdims=True)
            weights = jnp.exp2((scores - top) * scale).astype(bf16)
            mixed = jnp.dot(weights, values_by_head[head], preferred_element_type=f32)
            at = head // group
            other = (at + 1) % (width // LANES)
            total = mixed[:, other * LANES:(other + 1) * LANES]
            piece = mixed[:, at * LANES:(at + 1) * LANES]
            halves[at] = jnp.where(lane // HD == head % group, piece / total, halves[at])
            masses = jnp.where(lane // ROWS == head, total, masses)
            tops = jnp.where(lane // ROWS == head, top, tops)
        back[phase, pl.ds(start, devices)] = (
            jnp.concatenate(halves, axis=1).astype(bf16).reshape(devices, ROWS, width)
        )
        logs = tops * scale + jnp.log2(masses)
        logs = jnp.where(lane % ROWS == iota((TILE, LANES), 0) % ROWS, logs, 0.0)
        mass_back[phase, pl.ds(start, devices)] = jnp.sum(
            logs.reshape(devices, ROWS, LANES), axis=1, keepdims=True
        )

    @pl.loop(0, phases)
    def _(phase):
        all_copies(phase, *queries_out).wait_recv()
        recv[phase, me] = send[phase, me]

        @pl.loop(0, slots // TILE)
        def _(tile):
            attend(phase, tile)

        @pl.loop(1, n)
        def _(index):
            copy_to(index, phase, *answers_out).start()
            copy_to(index, phase, *masses_out).start()

    spread = (iota((LANES, width), 0) // ROWS == iota((LANES, width), 1) // HD).astype(f32).astype(bf16)
    own_lane = iota((n, ROWS, LANES), 2) % ROWS == iota((n, ROWS, LANES), 1)

    @pl.loop(0, phases)
    def _(phase):
        all_copies(phase, *answers_out).wait_recv()
        all_copies(phase, *masses_out).wait_recv()
        answer[phase, me] = back[phase, me]
        mass_answer[phase, me] = mass_back[phase, me]
        outs = answer[phase].reshape(slots, width)
        rest = jnp.where(own_lane, mass_answer[phase], 0.0).reshape(slots, LANES)
        columns = [outs]
        for _ in range(3):
            part = rest.astype(bf16)
            columns.append(part)
            rest = rest - part.astype(f32)
        for local in range(per_phase):
            step = phase * per_phase + local
            pos = pos_ref[step]
            places = iota((slots, nq), 0)
            match = jnp.concatenate(
                [(places == pos[0:1, :]).astype(f32), (places == pos[1:2, :]).astype(f32)], axis=1
            ).astype(bf16)
            picked = [
                lax.dot_general(match, c, (((0,), (0,)), ((), ())), preferred_element_type=f32)
                for c in columns
            ]
            logs = sum(
                jnp.dot(part.astype(bf16), spread, preferred_element_type=f32)
                for part in picked[1:]
            )
            share = 1.0 / (1.0 + jnp.exp2(logs[nq:] - logs[:nq]))
            merged = picked[0][nq:] + share * (picked[0][:nq] - picked[0][nq:])
            out_ref[step] = merged.astype(bf16)

    @pl.loop(0, phases)
    def _(phase):
        all_copies(phase, *queries_out).wait_send()
        all_copies(phase, *answers_out).wait_send()
        all_copies(phase, *masses_out).wait_send()


def body(ncol, n, queries, probes, keys, values, bucket_home, bucket_rows):
    steps, nq, width = queries.shape
    cap = max(1, 4 * nq // n)
    per_phase = min(steps, max(1, ROWS // cap))
    phases = steps // per_phase
    key_rows = keys.shape[1]
    heads = width // HD
    dims = (n, ncol, steps, nq, width, cap, per_phase, phases)
    vmem = pl.BlockSpec(memory_space=pltpu.VMEM)
    block = pltpu.VMEM((phases, n, ROWS, width), bf16)
    mass = pltpu.VMEM((phases, n, 1, LANES), f32)
    slots = phases * n * ROWS
    return pl.pallas_call(
        functools.partial(kernel, dims),
        out_shape=jax.ShapeDtypeStruct((steps, nq, width), bf16),
        in_specs=[vmem] * 6,
        out_specs=vmem,
        scratch_shapes=[
            pltpu.VMEM((heads, width, key_rows), bf16),
            pltpu.VMEM((heads, key_rows, width), bf16),
            pltpu.VMEM((steps, 2, nq), jnp.int32),
            block, block, block, block, mass, mass,
        ] + [pltpu.SemaphoreType.DMA((phases,))] * 6,
        compiler_params=pltpu.CompilerParams(
            collective_id=0, has_side_effects=True, vmem_limit_bytes=56 * 1024 * 1024
        ),
        cost_estimate=pl.CostEstimate(
            flops=4 * slots * key_rows * width * heads,
            bytes_accessed=4 * key_rows * width,
            transcendentals=slots * key_rows * heads,
        ),
    )(
        queries,
        jnp.transpose(probes, (0, 2, 1)),
        bucket_home.reshape(1, n),
        bucket_rows.reshape(1, n),
        keys[0],
        values[0],
    )


def solution(mesh):
    ncol = mesh.shape["col"]
    n = mesh.shape["row"] * ncol
    return jax.shard_map(
        functools.partial(body, ncol, n),
        mesh=mesh,
        in_specs=(
            P(None, ("row", "col"), None),
            P(None, ("row", "col"), None),
            P(("row", "col"), None, None),
            P(("row", "col"), None, None),
            P(),
            P(),
        ),
        out_specs=P(None, ("row", "col"), None),
        check_vma=False,
    )
```

time: 277 us -> 59.4 us (0.21)
  starting transfers between devices: 125 us -> 0 us
  waiting for transfers between devices: 65.1 us -> 0 us
  local copies, waits for them, and re-layouts: 59.2 us -> 1.67 us
  Pallas kernels: 0 us -> 57.5 us
  other arithmetic: 14.7 us -> 0 us
  loops' own time: 5.4 us -> 0 us
  matrix products: 4.96 us -> 0 us
    all_to_all x12 -> x0, starting transfers between devices: 125 us -> none  [the longest x4 57.2 us: return_answers(): lax.all_to_all(masses, ('row', 'col'), split_axis=0, concat_axis=0, tiled...]
    all_to_all x12 -> x0, waiting for transfers between devices: 65.1 us -> none  [the longest x4 36.7 us: return_answers(): lax.all_to_all(partials, ('row', 'col'), split_axis=0, concat_axis=0, til...]
    pallas_call x0 -> x1, Pallas kernels: none -> 57.5 us  [body(): pl.pallas_call(functools.partial(kernel, dims), out_shape=jax.ShapeDtypeS...]
    another operation x28 -> x0, local copies, waits for them, and re-layouts: 18.7 us -> none  [the longest x4 11 us: body(): partials = own_out.reshape(bucket_count, capacity, width)]
    scatter x4 -> x0, local copies, waits for them, and re-layouts: 8.58 us -> none  [body(): outgoing = jnp.zeros((bucket_count * capacity, width), jnp.bfloat16).at[f...]
    div x4 -> x0, local copies, waits for them, and re-layouts: 7.95 us -> none  [attend_blocks(): weighted / safe_mass[:, :, None]]
    gather x8 -> x0, local copies, waits for them, and re-layouts: 6.79 us -> none  [the longest x4 3.87 us: body(): gathered_out = back_out[first_pos].reshape(per_device, 2, H, HD)]
    another operation x4 -> x0, loops' own time: 5.4 us -> none  [attend_blocks(): lax.fori_loop(0, block_count, one_block, start_state)]
  transfers between devices with their start and end apart: 12 -> 0, of which waited for: 11 -> 0; matrix products, arithmetic and copies ran while one was open for 24% -> 0% of each run, Pallas kernels for 0% -> 0%
where the time goes in v1:
time: 59.4 us; the launch traced here: 59.2 us
  Pallas kernels  57.5 us (97%)
  local copies, waits for them, and re-layouts  1.67 us (3%)
    pallas_call x1, Pallas kernels, body(): pl.pallas_call(functools.partial(kernel, dims), out_shape=jax.ShapeDtypeS...  57.5 us
    unnamed x1, local copies, waits for them, and re-layouts  1.67 us

profile of v1, /device:TPU:0, one launch (start us, length us, event | category | flops | bytes accessed | tf_op | source)
XLA Modules:
  0.0 59.2 jit_solution(14461336203348290016)
XLA Ops:
  0.0 57.5 %shard_map.64 = bf16[4,128,256]{2,1,0:T(8,128)(2,1)} custom-call(bf16[4,128,256]{2,1,0:T(8,128)(2,1)} %q_ref.1, s32[4,2,128]{2,1,0:T(2,128)} %bitcast.7, s32[1,32]{1,0:T(1,128)} %bitcast.8, s32[1,32]{1,0:T(1,128)} %bitcast.9, bf16[1024,256]{1,0:T(8,128)(2,1)} %bitcast.5, bf16[1024,256]{1,0:T(8,128)(2,1)} %bitcast.6), custom_call_target="tpu_custom_call" | custom-call | flops 17179869184 | bytes 1048576 | tf_op jit(solution)/shard_map/pallas_call | solution.py:226
  57.5 1.7 %copy.8 = bf16[4,128,256]{2,1,0:T(8,128)(2,1)} copy(bf16[4,128,256]{2,1,0:T(8,128)(2,1)} %shard_map.64) | data formatting | bytes 524288

commit v2 on v1

--- a/solution.py
+++ b/solution.py
@@ -101,56 +101,58 @@
             total = part if total is None else total + part
         send[phase] = total.astype(bf16).reshape(n, ROWS, width)
 
-    for phase in range(phases):
-        arrange(phase)
-        if phase == 0:
-            pl.semaphore_wait(barrier, n - 1)
-
+    def send_queries(phase):
         @pl.loop(1, n)
         def _(index):
             copy_to(index, phase, *queries_out).start()
 
+    arrange(0)
+    pl.semaphore_wait(barrier, n - 1)
+    send_queries(0)
+
+    @pl.loop(1, phases)
+    def _(phase):
+        arrange(phase)
+        send_queries(phase)
+
     mine = jnp.sum(jnp.where(home_row == me, rows_ref[...], 0), axis=1, keepdims=True)
     valid = iota((key_rows, width), 0) < mine
     keys_all = k_ref[...].astype(f32)
-    keys_all = jnp.where(valid, keys_all, keys_all[0:1, :]).T
-    values_all = jnp.where(valid, v_ref[...].astype(f32), 0.0)
-    counted = jnp.where(valid, 1.0, 0.0)
+    keys_all = jnp.where(valid, keys_all, keys_all[0:1, :])
+    values_all = jnp.where(valid, v_ref[...].astype(f32), 0.0).T
+    counted = (iota((ROWS, key_rows), 1) < mine).astype(f32)
     for head in range(heads):
         keys_by_head[head] = jnp.where(
-            iota((width, key_rows), 0) // HD == head, keys_all, 0.0
+            iota((key_rows, width), 1) // HD == head, keys_all, 0.0
         ).astype(bf16)
-        values_by_head[head] = jnp.where(
-            iota((key_rows, width), 1) // HD == head, values_all, counted
+        values_by_head[head] = jnp.concatenate(
+            [values_all[head * HD:(head + 1) * HD], counted], axis=0
         ).astype(bf16)
-
-    lane = iota((TILE, LANES), 1)
-    group = LANES // HD
 
     def attend(phase, tile):
         devices = TILE // ROWS
         start = pl.multiple_of(tile * devices, devices)
         queries = recv[phase, pl.ds(start, devices)].reshape(TILE, width)
-        halves = [jnp.zeros((TILE, LANES), f32) for _ in range(width // LANES)]
-        masses = jnp.ones((TILE, LANES), f32)
-        tops = jnp.zeros((TILE, LANES), f32)
+        queries = queries.astype(f32).T.astype(bf16)
+        pieces, logs = [], []
+        following = jnp.dot(keys_by_head[0], queries, preferred_element_type=f32)
         for head in range(heads):
-            scores = jnp.dot(queries, keys_by_head[head], preferred_element_type=f32)
-            top = jnp.max(scores, axis=1, keepdims=True)
+            scores = following
+            if head + 1 < heads:
+                following = jnp.dot(keys_by_head[head + 1], queries, preferred_element_type=f32)
+            top = jnp.max(scores, axis=0, keepdims=True)
             weights = jnp.exp2((scores - top) * scale).astype(bf16)
-            mixed = jnp.dot(weights, values_by_head[head], preferred_element_type=f32)
-            at = head // group
-            other = (at + 1) % (width // LANES)
-            total = mixed[:, other * LANES:(other + 1) * LANES]
-            piece = mixed[:, at * LANES:(at + 1) * LANES]
-            halves[at] = jnp.where(lane // HD == head % group, piece / total, halves[at])
-            masses = jnp.where(lane // ROWS == head, total, masses)
-            tops = jnp.where(lane // ROWS == head, top, tops)
+            mixed = jnp.dot(values_by_head[head], weights, preferred_element_type=f32)
+            total = mixed[HD:HD + 1]
+            pieces.append(mixed[:HD] * (1.0 / total))
+            logs.append(jnp.broadcast_to(top * scale + jnp.log2(total), (ROWS, TILE)))
         back[phase, pl.ds(start, devices)] = (
-            jnp.concatenate(halves, axis=1).astype(bf16).reshape(devices, ROWS, width)
-        )
-        logs = tops * scale + jnp.log2(masses)
-        logs = jnp.where(lane % ROWS == iota((TILE, LANES), 0) % ROWS, logs, 0.0)
+            jnp.concatenate(pieces, axis=0).T.astype(bf16).reshape(devices, ROWS, width)
+        )
+        logs = jnp.concatenate(logs, axis=0).T
+        logs = jnp.where(
+            iota((TILE, LANES), 1) % ROWS == iota((TILE, LANES), 0) % ROWS, logs, 0.0
+        )
         mass_back[phase, pl.ds(start, devices)] = jnp.sum(
             logs.reshape(devices, ROWS, LANES), axis=1, keepdims=True
         )
@@ -229,8 +231,8 @@
         in_specs=[vmem] * 6,
         out_specs=vmem,
         scratch_shapes=[
-            pltpu.VMEM((heads, width, key_rows), bf16),
             pltpu.VMEM((heads, key_rows, width), bf16),
+            pltpu.VMEM((heads, HD + ROWS, key_rows), bf16),
             pltpu.VMEM((steps, 2, nq), jnp.int32),
             block, block, block, block, mass, mass,
         ] + [pltpu.SemaphoreType.DMA((phases,))] * 6,

time: 59.4 us -> 60.1 us (1.012)
  Pallas kernels: 57.5 us -> 58.3 us
    pallas_call x1, Pallas kernels: 57.5 us -> 58.3 us  [body(): pl.pallas_call(functools.partial(kernel, dims), out_shape=jax.ShapeDtypeS...]
where the time goes in v2:
time: 60.1 us; the launch traced here: 60 us
  Pallas kernels  58.3 us (97%)
  local copies, waits for them, and re-layouts  1.67 us (3%)
    pallas_call x1, Pallas kernels, body(): pl.pallas_call(functools.partial(kernel, dims), out_shape=jax.ShapeDtypeS...  58.3 us
    unnamed x1, local copies, waits for them, and re-layouts  1.67 us

profile of v2, /device:TPU:0, one launch (start us, length us, event | category | flops | bytes accessed | tf_op | source)
XLA Modules:
  0.0 60.0 jit_solution(2690211644373931212)
XLA Ops:
  0.0 58.3 %shard_map.64 = bf16[4,128,256]{2,1,0:T(8,128)(2,1)} custom-call(bf16[4,128,256]{2,1,0:T(8,128)(2,1)} %q_ref.1, s32[4,2,128]{2,1,0:T(2,128)} %bitcast.7, s32[1,32]{1,0:T(1,128)} %bitcast.8, s32[1,32]{1,0:T(1,128)} %bitcast.9, bf16[1024,256]{1,0:T(8,128)(2,1)} %bitcast.5, bf16[1024,256]{1,0:T(8,128)(2,1)} %bitcast.6), custom_call_target="tpu_custom_call" | custom-call | flops 17179869184 | bytes 1048576 | tf_op jit(solution)/shard_map/pallas_call | solution.py:228
  58.3 1.7 %copy.8 = bf16[4,128,256]{2,1,0:T(8,128)(2,1)} copy(bf16[4,128,256]{2,1,0:T(8,128)(2,1)} %shard_map.64) | data formatting | bytes 524288

commit v3 on v2

v3 whole, which is shorter than its diff:
```python
import functools
import math

import jax
import jax.numpy as jnp
from jax import lax
from jax.experimental import pallas as pl
from jax.experimental.pallas import tpu as pltpu
from jax.sharding import PartitionSpec as P

HD = 32
LANES = 128
ROWS = 16
TILE = 256
MESH = pl.DeviceIdType.MESH
bf16 = jnp.bfloat16
f32 = jnp.float32


def iota(shape, dim):
    return lax.broadcasted_iota(jnp.int32, shape, dim)


def kernel(
    dims, q_ref, probe_ref, home_ref, rows_ref, k_ref, v_ref, out_ref,
    keys_by_head, values_by_head, pos_ref, far_q, far_probe,
    send, recv, back, answer, mass_back, mass_answer, half_out, far_out, half_mass, far_mass,
    send_sem, recv_sem, back_sem, answer_sem, mass_back_sem, mass_answer_sem,
    q_sem, far_q_sem, half_sem, far_sem, half_mass_sem, far_mass_sem, probe_sem, far_probe_sem,
):
    n, ncol, steps, nq, width, cap, per_phase, phases = dims
    heads = width // HD
    key_rows = k_ref.shape[0]
    hcol = ncol // 2
    m = n // 2
    slots = m * ROWS
    scale = math.log2(math.e) / math.sqrt(HD)
    row, col = lax.axis_index("row"), lax.axis_index("col")
    device = row * ncol + col
    half = col // hcol
    me = row * hcol + lax.rem(col, hcol)
    mirror = (row, lax.rem(col + hcol, ncol))

    def peer(index):
        other = lax.rem(me + index, m)
        return other, (other // hcol, half * hcol + lax.rem(other, hcol))

    barrier = pltpu.get_barrier_semaphore()
    pl.semaphore_signal(barrier, inc=1, device_id=mirror, device_id_type=MESH)

    @pl.loop(1, m)
    def _(index):
        _, where = peer(index)
        pl.semaphore_signal(barrier, inc=1, device_id=where, device_id_type=MESH)

    def copy_to(index, unit, source, target, source_sem, target_sem):
        other, where = peer(index)
        return pltpu.make_async_remote_copy(
            src_ref=source.at[unit, other],
            dst_ref=target.at[unit, me],
            send_sem=source_sem.at[unit],
            recv_sem=target_sem.at[unit],
            device_id=where,
            device_id_type=MESH,
        )

    def all_copies(unit, source, target, source_sem, target_sem):
        _, where = peer(1)
        return pltpu.make_async_remote_copy(
            src_ref=source.at[unit, pl.ds(0, m - 1)],
            dst_ref=target.at[unit, pl.ds(0, m - 1)],
            send_sem=source_sem.at[unit],
            recv_sem=target_sem.at[unit],
            device_id=where,
            device_id_type=MESH,
        )

    def mirrored(phase, source, target, source_sem, target_sem):
        part = pl.ds(phase * per_phase, per_phase)
        return pltpu.make_async_remote_copy(
            src_ref=source.at[part],
            dst_ref=target.at[part],
            send_sem=source_sem.at[phase],
            recv_sem=target_sem.at[phase],
            device_id=mirror,
            device_id_type=MESH,
        )

    queries_out = (send, recv, send_sem, recv_sem)
    answers_out = (back, answer, back_sem, answer_sem)
    masses_out = (mass_back, mass_answer, mass_back_sem, mass_answer_sem)
    far_queries = (q_ref, far_q, q_sem, far_q_sem)
    far_answers = (half_out, far_out, half_sem, far_sem)
    far_masses = (half_mass, far_mass, half_mass_sem, far_mass_sem)
    far_probes = pltpu.make_async_remote_copy(
        src_ref=probe_ref, dst_ref=far_probe, send_sem=probe_sem.at[0], recv_sem=far_probe_sem.at[0],
        device_id=mirror, device_id_type=MESH,
    )

    home_row = home_ref[...]
    home_col = home_row % ncol
    base_row = jnp.where(
        home_col // hcol == half, (home_row // ncol * hcol + home_col % hcol) * ROWS, -(1 << 20)
    )
    diagonal = iota((n, n), 0) == iota((n, n), 1)
    base = jnp.sum(jnp.where(diagonal, base_row, 0), axis=1, keepdims=True).astype(f32)
    before = (iota((nq, nq), 0) < iota((nq, nq), 1)).astype(bf16)

    def slot_rows(ids, local):
        first = (iota((n, nq), 0) == ids[0:1, :]).astype(f32)
        second = (iota((n, nq), 0) == ids[1:2, :]).astype(f32)
        both = jnp.concatenate([first, second], axis=0).astype(bf16)
        earlier = jnp.dot(both, before, preferred_element_type=f32)
        offset = jnp.sum(first, axis=1, keepdims=True)
        order_first = jnp.sum(first * (earlier[:n] + base), axis=0, keepdims=True)
        order_second = jnp.sum(second * (earlier[n:] + offset + base), axis=0, keepdims=True)
        return jnp.concatenate([order_first, order_second], axis=0).astype(jnp.int32) + local * cap

    def send_queries(group, phase):
        total = None
        for local in range(per_phase):
            step = phase * per_phase + local
            pos = slot_rows((far_probe if group else probe_ref)[step], local)
            pos_ref[group, step] = pos
            places = iota((slots, nq), 0)
            match = ((places == pos[0:1, :]) | (places == pos[1:2, :])).astype(f32).astype(bf16)
            part = jnp.dot(match, (far_q if group else q_ref)[step], preferred_element_type=f32)
            total = part if total is None else total + part
        send[2 * phase + group] = total.astype(bf16).reshape(m, ROWS, width)

        @pl.loop(1, m)
        def _(index):
            copy_to(index, 2 * phase + group, *queries_out).start()

    pl.semaphore_wait(barrier, m)
    far_probes.start()
    for phase in range(phases):
        mirrored(phase, *far_queries).start()

    @pl.loop(0, phases)
    def _(phase):
        send_queries(0, phase)

    mine = jnp.sum(jnp.where(home_row == device, rows_ref[...], 0), axis=1, keepdims=True)
    valid = iota((key_rows, width), 0) < mine
    keys_all = k_ref[...].astype(f32)
    keys_all = jnp.where(valid, keys_all, keys_all[0:1, :])
    values_all = jnp.where(valid, v_ref[...].astype(f32), 0.0).T
    counted = (iota((ROWS, key_rows), 1) < mine).astype(f32)
    for head in range(heads):
        keys_by_head[head] = jnp.where(
            iota((key_rows, width), 1) // HD == head, keys_all, 0.0
        ).astype(bf16)
        values_by_head[head] = jnp.concatenate(
            [values_all[head * HD:(head + 1) * HD], counted], axis=0
        ).astype(bf16)

    def attend(unit, tile):
        devices = TILE // ROWS
        start = pl.multiple_of(tile * devices, devices)
        queries = recv[unit, pl.ds(start, devices)].reshape(TILE, width)
        queries = queries.astype(f32).T.astype(bf16)
        pieces, logs = [], []
        following = jnp.dot(keys_by_head[0], queries, preferred_element_type=f32)
        for head in range(heads):
            scores = following
            if head + 1 < heads:
                following = jnp.dot(keys_by_head[head + 1], queries, preferred_element_type=f32)
            top = jnp.max(scores, axis=0, keepdims=True)
            weights = jnp.exp2((scores - top) * scale).astype(bf16)
            mixed = jnp.dot(values_by_head[head], weights, preferred_element_type=f32)
            total = mixed[HD:HD + 1]
            pieces.append(mixed[:HD] * (1.0 / total))
            logs.append(jnp.broadcast_to(top * scale + jnp.log2(total), (ROWS, TILE)))
        back[unit, pl.ds(start, devices)] = (
            jnp.concatenate(pieces, axis=0).T.astype(bf16).reshape(devices, ROWS, width)
        )
        logs = jnp.concatenate(logs, axis=0).T
        logs = jnp.where(
            iota((TILE, LANES), 1) % ROWS == iota((TILE, LANES), 0) % ROWS, logs, 0.0
        )
        mass_back[unit, pl.ds(start, devices)] = jnp.sum(
            logs.reshape(devices, ROWS, LANES), axis=1, keepdims=True
        )

    spread = (iota((LANES, width), 0) // ROWS == iota((LANES, width), 1) // HD).astype(f32).astype(bf16)
    own_lane = iota((m, ROWS, LANES), 2) % ROWS == iota((m, ROWS, LANES), 1)
    ones = jnp.ones((slots, LANES), bf16)

    def combine(out_a, log_a, out_b, log_b):
        top = jnp.maximum(log_a, log_b)
        share_a, share_b = jnp.exp2(log_a - top), jnp.exp2(log_b - top)
        total = share_a + share_b
        return (share_a * out_a + share_b * out_b) / total, top + jnp.log2(total)

    def half_answers(group, phase):
        unit = 2 * phase + group
        all_copies(unit, *answers_out).wait_recv()
        all_copies(unit, *masses_out).wait_recv()
        answer[unit, me] = back[unit, me]
        mass_answer[unit, me] = mass_back[unit, me]
        outs = answer[unit].reshape(slots, width)
        rest = jnp.where(own_lane, mass_answer[unit], 0.0).reshape(slots, LANES)
        columns = [outs, ones]
        for _ in range(3):
            part = rest.astype(bf16)
            columns.append(part)
            rest = rest - part.astype(f32)
        results = []
        for local in range(per_phase):
            pos = pos_ref[group, phase * per_phase + local]
            places = iota((slots, nq), 0)
            match = jnp.concatenate(
                [(places == pos[0:1, :]).astype(f32), (places == pos[1:2, :]).astype(f32)], axis=1
            ).astype(bf16)
            picked = [
                lax.dot_general(match, c, (((0,), (0,)), ((), ())), preferred_element_type=f32)
                for c in columns
            ]
            logs = sum(
                jnp.dot(part.astype(bf16), spread, preferred_element_type=f32)
                for part in picked[2:]
            )
            there = jnp.concatenate([picked[1]] * (width // LANES), axis=1)
            logs = jnp.where(there > 0.5, logs, -1e30)
            results.append(combine(picked[0][:nq], logs[:nq], picked[0][nq:], logs[nq:]))
        return results

    def answer_mirror(phase):
        for local, (out, log) in enumerate(half_answers(1, phase)):
            step = phase * per_phase + local
            turned = log.T
            half_out[step] = out.astype(bf16)
            half_mass[step] = jnp.concatenate(
                [turned[head * HD:head * HD + 1] for head in range(heads)], axis=0
            )
        mirrored(phase, *far_answers).start()
        mirrored(phase, *far_masses).start()

    def forward(phase):
        mirrored(phase, *far_queries).wait_recv()
        send_queries(1, phase)

    far_probes.wait_recv()
    forward(0)

    @pl.loop(0, 2 * phases)
    def _(turn):
        phase = turn // 2
        odd = turn % 2
        group = jnp.where(phase == 0, odd, 1 - odd)
        unit = 2 * phase + group

        @pl.when((odd == 0) & (phase + 1 < phases))
        def _():
            forward(phase + 1)

        all_copies(unit, *queries_out).wait_recv()
        recv[unit, me] = send[unit, me]

        @pl.loop(0, slots // TILE)
        def _(tile):
            attend(unit, tile)

        @pl.loop(1, m)
        def _(index):
            copy_to(index, unit, *answers_out).start()
            copy_to(index, unit, *masses_out).start()

        @pl.when((odd == 0) & (phase > 0))
        def _():
            answer_mirror(phase - 1)

    answer_mirror(phases - 1)

    @pl.loop(0, phases)
    def _(phase):
        near = half_answers(0, phase)
        mirrored(phase, *far_answers).wait_recv()
        mirrored(phase, *far_masses).wait_recv()
        for local, (out, log) in enumerate(near):
            step = phase * per_phase + local
            other = far_mass[step]
            other = jnp.concatenate(
                [jnp.broadcast_to(other[head:head + 1], (HD, nq)) for head in range(heads)], axis=0
            ).T
            out_ref[step] = combine(out, log, far_out[step].astype(f32), other)[0].astype(bf16)

    far_probes.wait_send()

    @pl.loop(0, phases)
    def _(phase):
        mirrored(phase, *far_queries).wait_send()
        mirrored(phase, *far_answers).wait_send()
        mirrored(phase, *far_masses).wait_send()

    @pl.loop(0, 2 * phases)
    def _(unit):
        all_copies(unit, *queries_out).wait_send()
        all_copies(unit, *answers_out).wait_send()
        all_copies(unit, *masses_out).wait_send()


def body(ncol, n, queries, probes, keys, values, bucket_home, bucket_rows):
    steps, nq, width = queries.shape
    cap = max(1, 4 * nq // n)
    per_phase = min(steps, max(1, ROWS // cap))
    phases = steps // per_phase
    key_rows = keys.shape[1]
    heads = width // HD
    dims = (n, ncol, steps, nq, width, cap, per_phase, phases)
    vmem = pl.BlockSpec(memory_space=pltpu.VMEM)
    block = pltpu.VMEM((2 * phases, n // 2, ROWS, width), bf16)
    mass = pltpu.VMEM((2 * phases, n // 2, 1, LANES), f32)
    whole = pltpu.VMEM((steps, nq, width), bf16)
    whole_mass = pltpu.VMEM((steps, heads, nq), f32)
    dma = pltpu.SemaphoreType.DMA
    slots = phases * n * ROWS
    return pl.pallas_call(
        functools.partial(kernel, dims),
        out_shape=jax.ShapeDtypeStruct((steps, nq, width), bf16),
        in_specs=[vmem] * 6,
        out_specs=vmem,
        scratch_shapes=[
            pltpu.VMEM((heads, key_rows, width), bf16),
            pltpu.VMEM((heads, HD + ROWS, key_rows), bf16),
            pltpu.VMEM((2, steps, 2, nq), jnp.int32),
            whole,
            pltpu.VMEM((steps, 2, nq), jnp.int32),
            block, block, block, block, mass, mass, whole, whole, whole_mass, whole_mass,
        ] + [dma((2 * phases,))] * 6 + [dma((phases,))] * 6 + [dma((1,))] * 2,
        compiler_params=pltpu.CompilerParams(
            collective_id=0, has_side_effects=True, vmem_limit_bytes=56 * 1024 * 1024
        ),
        cost_estimate=pl.CostEstimate(
            flops=4 * slots * key_rows * width * heads,
            bytes_accessed=4 * key_rows * width,
            transcendentals=slots * key_rows * heads,
        ),
    )(
        queries,
        jnp.transpose(probes, (0, 2, 1)),
        bucket_home.reshape(1, n),
        bucket_rows.reshape(1, n),
        keys[0],
        values[0],
    )


def solution(mesh):
    ncol = mesh.shape["col"]
    n = mesh.shape["row"] * ncol
    return jax.shard_map(
        functools.partial(body, ncol, n),
        mesh=mesh,
        in_specs=(
            P(None, ("row", "col"), None),
            P(None, ("row", "col"), None),
            P(("row", "col"), None, None),
            P(("row", "col"), None, None),
            P(),
            P(),
        ),
        out_specs=P(None, ("row", "col"), None),
        check_vma=False,
    )
```

time: 60.1 us -> 62.3 us (1.037)
  Pallas kernels: 58.3 us -> 60.5 us
    pallas_call x1, Pallas kernels: 58.3 us -> 60.5 us  [body(): pl.pallas_call(functools.partial(kernel, dims), out_shape=jax.ShapeDtypeS...]
where the time goes in v3:
time: 62.3 us; the launch traced here: 62.2 us
  Pallas kernels  60.5 us (97%)
  local copies, waits for them, and re-layouts  1.67 us (3%)
    pallas_call x1, Pallas kernels, body(): pl.pallas_call(functools.partial(kernel, dims), out_shape=jax.ShapeDtypeS...  60.5 us
    unnamed x1, local copies, waits for them, and re-layouts  1.67 us

profile of v3, /device:TPU:0, one launch (start us, length us, event | category | flops | bytes accessed | tf_op | source)
XLA Modules:
  0.0 62.2 jit_solution(12325714253082870797)
XLA Ops:
  0.0 60.5 %shard_map.64 = bf16[4,128,256]{2,1,0:T(8,128)(2,1)} custom-call(bf16[4,128,256]{2,1,0:T(8,128)(2,1)} %q_ref.1, s32[4,2,128]{2,1,0:T(2,128)} %bitcast.7, s32[1,32]{1,0:T(1,128)} %bitcast.8, s32[1,32]{1,0:T(1,128)} %bitcast.9, bf16[1024,256]{1,0:T(8,128)(2,1)} %bitcast.5, bf16[1024,256]{1,0:T(8,128)(2,1)} %bitcast.6), custom_call_target="tpu_custom_call" | custom-call | flops 17179869184 | bytes 1048576 | tf_op jit(solution)/shard_map/pallas_call | solution.py:319
  60.5 1.7 %copy.8 = bf16[4,128,256]{2,1,0:T(8,128)(2,1)} copy(bf16[4,128,256]{2,1,0:T(8,128)(2,1)} %shard_map.64) | data formatting | bytes 524288

commit v4 on v2

--- a/solution.py
+++ b/solution.py
@@ -12,6 +12,7 @@
 LANES = 128
 ROWS = 16
 TILE = 256
+SHIFT = 1.5
 MESH = pl.DeviceIdType.MESH
 bf16 = jnp.bfloat16
 f32 = jnp.float32
@@ -23,8 +24,7 @@
 
 def kernel(
     dims, q_ref, probe_ref, home_ref, rows_ref, k_ref, v_ref, out_ref,
-    keys_by_head, values_by_head, pos_ref, send, recv, back, answer, mass_back, mass_answer,
-    send_sem, recv_sem, back_sem, answer_sem, mass_back_sem, mass_answer_sem,
+    keys_by_head, values_by_head, pos_ref, send, recv, back, answer, send_sem, recv_sem, back_sem, answer_sem,
 ):
     n, ncol, steps, nq, width, cap, per_phase, phases = dims
     heads = width // HD
@@ -68,7 +68,6 @@
 
     queries_out = (send, recv, send_sem, recv_sem)
     answers_out = (back, answer, back_sem, answer_sem)
-    masses_out = (mass_back, mass_answer, mass_back_sem, mass_answer_sem)
 
     home_row = home_ref[...]
     diagonal = iota((n, n), 0) == iota((n, n), 1)
@@ -140,21 +139,21 @@
             scores = following
             if head + 1 < heads:
                 following = jnp.dot(keys_by_head[head + 1], queries, preferred_element_type=f32)
-            top = jnp.max(scores, axis=0, keepdims=True)
-            weights = jnp.exp2((scores - top) * scale).astype(bf16)
+            top = jnp.max(scores.reshape(-1, LANES, TILE), axis=0)
+            top = jnp.max(top, axis=0, keepdims=True) * scale - SHIFT
+            weights = jnp.exp2((scores * scale - top).astype(bf16))
             mixed = jnp.dot(values_by_head[head], weights, preferred_element_type=f32)
             total = mixed[HD:HD + 1]
             pieces.append(mixed[:HD] * (1.0 / total))
-            logs.append(jnp.broadcast_to(top * scale + jnp.log2(total), (ROWS, TILE)))
+            logs.append(top + jnp.log2(total))
+        rest = jnp.concatenate(logs, axis=0)
+        for _ in range(3):
+            part = rest.astype(bf16).astype(f32)
+            pieces.append(part)
+            rest = rest - part
+        pieces.append(jnp.zeros((LANES - 3 * heads, TILE), f32))
         back[phase, pl.ds(start, devices)] = (
-            jnp.concatenate(pieces, axis=0).T.astype(bf16).reshape(devices, ROWS, width)
-        )
-        logs = jnp.concatenate(logs, axis=0).T
-        logs = jnp.where(
-            iota((TILE, LANES), 1) % ROWS == iota((TILE, LANES), 0) % ROWS, logs, 0.0
-        )
-        mass_back[phase, pl.ds(start, devices)] = jnp.sum(
-            logs.reshape(devices, ROWS, LANES), axis=1, keepdims=True
+            jnp.concatenate(pieces, axis=0).T.astype(bf16).reshape(devices, ROWS, width + LANES)
         )
 
     @pl.loop(0, phases)
@@ -169,24 +168,16 @@
         @pl.loop(1, n)
         def _(index):
             copy_to(index, phase, *answers_out).start()
-            copy_to(index, phase, *masses_out).start()
-
-    spread = (iota((LANES, width), 0) // ROWS == iota((LANES, width), 1) // HD).astype(f32).astype(bf16)
-    own_lane = iota((n, ROWS, LANES), 2) % ROWS == iota((n, ROWS, LANES), 1)
+
+    source = iota((LANES, width), 0)
+    spread = (source % heads == iota((LANES, width), 1) // HD) & (source < 3 * heads)
+    spread = spread.astype(f32).astype(bf16)
 
     @pl.loop(0, phases)
     def _(phase):
         all_copies(phase, *answers_out).wait_recv()
-        all_copies(phase, *masses_out).wait_recv()
         answer[phase, me] = back[phase, me]
-        mass_answer[phase, me] = mass_back[phase, me]
-        outs = answer[phase].reshape(slots, width)
-        rest = jnp.where(own_lane, mass_answer[phase], 0.0).reshape(slots, LANES)
-        columns = [outs]
-        for _ in range(3):
-            part = rest.astype(bf16)
-            columns.append(part)
-            rest = rest - part.astype(f32)
+        outs = answer[phase].reshape(slots, width + LANES)
         for local in range(per_phase):
             step = phase * per_phase + local
             pos = pos_ref[step]
@@ -194,23 +185,19 @@
             match = jnp.concatenate(
                 [(places == pos[0:1, :]).astype(f32), (places == pos[1:2, :]).astype(f32)], axis=1
             ).astype(bf16)
-            picked = [
-                lax.dot_general(match, c, (((0,), (0,)), ((), ())), preferred_element_type=f32)
-                for c in columns
-            ]
-            logs = sum(
-                jnp.dot(part.astype(bf16), spread, preferred_element_type=f32)
-                for part in picked[1:]
+            picked = lax.dot_general(
+                match, outs, (((0,), (0,)), ((), ())), preferred_element_type=f32
             )
+            logs = jnp.dot(picked[:, width:].astype(bf16), spread, preferred_element_type=f32)
+            picked = picked[:, :width]
             share = 1.0 / (1.0 + jnp.exp2(logs[nq:] - logs[:nq]))
-            merged = picked[0][nq:] + share * (picked[0][:nq] - picked[0][nq:])
+            merged = picked[nq:] + share * (picked[:nq] - picked[nq:])
             out_ref[step] = merged.astype(bf16)
 
     @pl.loop(0, phases)
     def _(phase):
         all_copies(phase, *queries_out).wait_send()
         all_copies(phase, *answers_out).wait_send()
-        all_copies(phase, *masses_out).wait_send()
 
 
 def body(ncol, n, queries, probes, keys, values, bucket_home, bucket_rows):
@@ -223,7 +210,7 @@
     dims = (n, ncol, steps, nq, width, cap, per_phase, phases)
     vmem = pl.BlockSpec(memory_space=pltpu.VMEM)
     block = pltpu.VMEM((phases, n, ROWS, width), bf16)
-    mass = pltpu.VMEM((phases, n, 1, LANES), f32)
+    wide = pltpu.VMEM((phases, n, ROWS, width + LANES), bf16)
     slots = phases * n * ROWS
     return pl.pallas_call(
         functools.partial(kernel, dims),
@@ -234,8 +221,8 @@
             pltpu.VMEM((heads, key_rows, width), bf16),
             pltpu.VMEM((heads, HD + ROWS, key_rows), bf16),
             pltpu.VMEM((steps, 2, nq), jnp.int32),
-            block, block, block, block, mass, mass,
-        ] + [pltpu.SemaphoreType.DMA((phases,))] * 6,
+            block, block, wide, wide,
+        ] + [pltpu.SemaphoreType.DMA((phases,))] * 4,
         compiler_params=pltpu.CompilerParams(
             collective_id=0, has_side_effects=True, vmem_limit_bytes=56 * 1024 * 1024
         ),

time: 60.1 us -> 68.6 us (1.14)
  Pallas kernels: 58.3 us -> 66.8 us
    pallas_call x1, Pallas kernels: 58.3 us -> 66.8 us  [body(): pl.pallas_call(functools.partial(kernel, dims), out_shape=jax.ShapeDtypeS...]
where the time goes in v4:
time: 68.6 us; the launch traced here: 68.5 us
  Pallas kernels  66.8 us (97%)
  local copies, waits for them, and re-layouts  1.67 us (2%)
    pallas_call x1, Pallas kernels, body(): pl.pallas_call(functools.partial(kernel, dims), out_shape=jax.ShapeDtypeS...  66.8 us
    unnamed x1, local copies, waits for them, and re-layouts  1.67 us

profile of v4, /device:TPU:0, one launch (start us, length us, event | category | flops | bytes accessed | tf_op | source)
XLA Modules:
  0.0 68.5 jit_solution(16592644242564791884)
XLA Ops:
  0.0 66.8 %shard_map.64 = bf16[4,128,256]{2,1,0:T(8,128)(2,1)} custom-call(bf16[4,128,256]{2,1,0:T(8,128)(2,1)} %q_ref.1, s32[4,2,128]{2,1,0:T(2,128)} %bitcast.7, s32[1,32]{1,0:T(1,128)} %bitcast.8, s32[1,32]{1,0:T(1,128)} %bitcast.9, bf16[1024,256]{1,0:T(8,128)(2,1)} %bitcast.5, bf16[1024,256]{1,0:T(8,128)(2,1)} %bitcast.6), custom_call_target="tpu_custom_call" | custom-call | flops 17179869184 | bytes 1048576 | tf_op jit(solution)/shard_map/pallas_call | solution.py:215
  66.8 1.7 %copy.8 = bf16[4,128,256]{2,1,0:T(8,128)(2,1)} copy(bf16[4,128,256]{2,1,0:T(8,128)(2,1)} %shard_map.64) | data formatting | bytes 524288
